TPU v7x, 32 devices: a whole 2x2x4 slice. The times are simulated.
32 devices in a mesh: grp: 2 (over y), mod: 4 (over z), dp: 4 (over x, core).
Axes of the slice: x: 2, y: 2, z: 4, core: 2. Of those that a mesh axis runs over, the one named last changes fastest.
Arguments:
- act_proj: bfloat16 [512, 64, 128], P(('grp', 'mod', 'dp')), parts along dimension 0, may hold values from -3 to 3
- grad_proj: bfloat16 [512, 64, 128], P(('grp', 'mod', 'dp')), parts along dimension 0, may hold values from -3 to 3
- lengths: int32 [512], P(('grp', 'mod', 'dp')), parts along dimension 0, may hold values from 1 to 64
- assignment: int32 [4], replicated, may hold values from 0 to 3, each once
Outputs:
- covariance: float32 [2048, 4, 1024], P(('grp', 'dp'), 'mod'), parts along dimension 0
There are 2 independent parts, one for each index of `grp`. A program takes and returns all parts, laid end to end along the dimension named above; an argument that names none is the same for every part. Nothing has to cross between parts.
Inputs may be any that keep to these rules, and one draw needn't show every extreme that they name: assignment is a permutation of the module positions.
All inputs are finite; a program needn't handle non-finite values.
Results may differ from a plain program's by a relative error of at most 0.0003.
Values may be sent and summed in bfloat16 or wider, within the bound.
A program may use at most 64 MiB of HBM per device.

v0:
```python
import jax
import jax.numpy as jnp
from jax import lax
from jax.sharding import PartitionSpec as P


def body(act_proj, grad_proj, lengths, assignment):
    ex_count, seq_len, width = act_proj.shape
    modules = assignment.shape[0]
    proj_rank = width // modules
    entries = proj_rank * proj_rank
    source = jnp.argsort(assignment)
    activations = act_proj.reshape(ex_count, seq_len, modules, proj_rank)
    gradients = grad_proj.reshape(ex_count, seq_len, modules, proj_rank)
    valid_tokens = lax.iota(jnp.int32, seq_len)[None, :] < lengths[:, None]
    gradients = jnp.where(valid_tokens[:, :, None, None], gradients, jnp.zeros((), jnp.bfloat16))
    activations = jnp.take(activations, source, axis=2)
    gradients = jnp.take(gradients, source, axis=2)
    local_grad = jnp.einsum(
        "etma,etmb->emab", gradients, activations, preferred_element_type=jnp.float32
    )
    local_grad = local_grad.reshape(ex_count, modules, entries)
    example_grad = lax.all_to_all(local_grad, "mod", split_axis=1, concat_axis=0, tiled=True)
    inverse_count = 1.0 / (example_grad.shape[0] * lax.axis_size("dp"))
    covariance = lax.psum_scatter(
        jnp.einsum("emi,emj->imj", example_grad, example_grad, precision=lax.Precision.HIGHEST),
        "dp",
        scatter_dimension=0,
        tiled=True,
    )
    return covariance * inverse_count


def solution(mesh):
    return jax.shard_map(
        body,
        mesh=mesh,
        in_specs=(
            P(("grp", "mod", "dp"), None, None),
            P(("grp", "mod", "dp"), None, None),
            P(("grp", "mod", "dp")),
            P(),
        ),
        out_specs=P(("grp", "dp"), "mod", None),
        check_vma=False,
    )
```

profile of v0, /device:TPU:0, one launch (start us, length us, event | category | flops | bytes accessed | tf_op | source)
XLA Modules:
  0.0 87.6 jit_solution(10236777162931244113)
XLA Ops:
  6.5 0.0 reduce-scatter.2.cloned.1.call-start
  6.5 1.4 %sort.17 = (s32[4]{0:T(128)}, s32[4]{0:T(128)S(1)}) sort(s32[4]{0:T(128)} %param.9, s32[4]{0:T(128)S(1)} %iota.11), dimensions={0}, to_apply=%region_0.0 | sort | flops 8 | bytes 64 | tf_op jit(solution)/shard_map/jit(argsort)/sort | solution.py:12
  7.9 0.7 iota_compare_fusion
  8.7 1.2 %copy.8 = bf16[16,64,128]{1,2,0:T(8,128)(2,1)S(1)} copy(bf16[16,64,128]{2,1,0:T(8,128)(2,1)} %param.6) | data formatting | bytes 524288 | tf_op args[0]
  9.9 1.2 %copy.7 = bf16[16,64,128]{1,2,0:T(8,128)(2,1)S(1)} copy(bf16[16,64,128]{2,1,0:T(8,128)(2,1)} %param.7) | data formatting | bytes 524288 | tf_op args[1]
  11.2 0.6 gather_fusion.1
  11.9 0.6 gather_fusion
  12.5 0.2 select_bitcast_fusion.1
  12.7 0.4 fusion
  13.1 0.5 reshape.46
  13.6 0.2 copy.11
  13.7 15.0 %all_to_all.15 = f32[16,4,1024]{2,0,1:T(8,128)S(1)} all-to-all(f32[16,4,1024]{2,0,1:T(8,128)S(1)} %copy.11), channel_id=1, replica_groups=mesh['grp'=2,'mod'=4,'dp'=4] {'mod'}, dimensions={1} | all-to-all | bytes 524288 | tf_op jit(solution)/shard_map/all_to_all | solution.py:23
  28.7 5.1 %convolution_bitcast_fusion = f32[1024,1,1024]{0,2,1:T(8,128)} fusion(f32[16,4,1024]{2,0,1:T(8,128)S(1)} %all_to_all.15), kind=kOutput, calls=%fused_computation.2 | convolution fusion | flops 805306368 | bytes 4456448 | tf_op jit(solution)/shard_map/emi,emj->imj/dot_general | solution.py:26
  33.8 0.0 reduce-scatter.2.cloned.1.call-update
  33.8 43.8 %reduce-scatter.2.cloned.1.call-done = f32[256,1,1024]{0,2,1:T(8,128)} async-done(((f32[1024,1,1024]{0,2,1:T(8,128)}), f32[256,1,1024]{0,2,1:T(8,128)}) %reduce-scatter.2.cloned.1.call-update) | async-done | bytes 1048592 | tf_op jit(solution)/shard_map/reduce_scatter | solution.py:25
  77.6 1.3 %broadcast_multiply_fusion = f32[256,1,1024]{0,2,1:T(8,128)S(1)} fusion(f32[256,1,1024]{0,2,1:T(8,128)} %reduce-scatter.2.cloned.1.call-done), kind=kLoop, calls=%fused_computation.8 | loop fusion | flops 262144 | bytes 2097152 | tf_op jit(solution)/shard_map/mul | solution.py:31
  78.9 1.9 %copy.12 = f32[256,1,1024]{2,1,0:T(1,128)} copy(f32[256,1,1024]{0,2,1:T(8,128)S(1)} %broadcast_multiply_fusion) | data formatting | bytes 2097152 | tf_op jit(solution)/shard_map/mul | solution.py:31
  (5 shorter events, 0.1 us)
Async XLA Ops:
  6.5 71.0 %reduce-scatter.2.cloned.1.call-start = ((), (), s32[]{:S(2)}) async-start(), calls=%async_computation.2 | async-start | bytes 5242880 | tf_op jit(solution)/shard_map/reduce_scatter | solution.py:25
Sparse Core Ops, SparseCore 0:
  33.9 43.5 reduce-scatter.1
where the time goes:
time: 87.9 us; the launch traced here: 87.6 us
  waiting for transfers between devices  43.8 us (50%)
  blocking collectives  15 us (17%)
  between operations  13.5 us (15%)
  local copies, waits for them, and re-layouts  6.3 us (7%)
  matrix products  5.44 us (6%)
  other arithmetic  3.65 us (4%)
    reduce_scatter x1, waiting for transfers between devices, body(): lax.psum_scatter(jnp.einsum('emi,emj->imj', example_grad, example_grad, p...  43.8 us
    all_to_all x1, blocking collectives, body(): lax.all_to_all(local_grad, 'mod', split_axis=1, concat_axis=0, tiled=True)  15 us
    dot_general x1, matrix products, body(): jnp.einsum('emi,emj->imj', example_grad, example_grad, precision=lax.Prec...  5.05 us
    unnamed x2, local copies, waits for them, and re-layouts  2.45 us
    mul x1, local copies, waits for them, and re-layouts, body(): return covariance * inverse_count  1.9 us
  transfers between devices with their start and end apart: 1, of which 1 were waited for; matrix products, arithmetic and copies ran while one was open for 0% of the time, Pallas kernels for 0%

commit v1 on v0

v1 whole, which is shorter than its diff:
```python
import functools

import jax
import jax.numpy as jnp
from jax import lax
from jax.experimental import pallas as pl
from jax.experimental.pallas import tpu as pltpu
from jax.sharding import PartitionSpec as P

MESH = pl.DeviceIdType.MESH
LANES = 128


def kernel(
    n_mod, n_dp, rank, lens_ref, assign_ref, act_hbm, grad_hbm, out_ref,
    act_v, grad_v, prod, coded, outbox, inbox, high, low,
    in_sem, z_send, z_recv, x_send, x_recv, c_send, c_recv, f_send, f_recv,
):
    ex, seq, width = act_v.shape
    entries = rank * rank
    tiles = entries // LANES
    per_tile = LANES // rank
    n_lo = 2 if n_dp % 2 == 0 else 1
    n_hi = n_dp // n_lo
    small = n_mod <= 8
    mod = lax.axis_index("mod")
    dp = lax.axis_index("dp")
    hi, lo = dp // n_lo, dp % n_lo
    mine = [pltpu.make_async_copy(act_hbm, act_v, in_sem.at[0]),
            pltpu.make_async_copy(grad_hbm, grad_v, in_sem.at[1])]
    for copy in mine:
        copy.start()

    mod_at = [lax.rem(mod + o, n_mod) for o in range(n_mod)]
    mod_from = [lax.rem(mod + n_mod - o, n_mod) for o in range(n_mod)]
    hi_at = [lax.rem(hi + h, n_hi) * n_lo + lo for h in range(n_hi)]
    hi_from = [lax.rem(hi + n_hi - h, n_hi) for h in range(n_hi)]

    barrier = pltpu.get_barrier_semaphore()
    for o in range(1, n_mod):
        pl.semaphore_signal(barrier, inc=1, device_id={"mod": mod_at[o]}, device_id_type=MESH)
    for h in range(1, n_hi):
        pl.semaphore_signal(barrier, inc=1, device_id={"dp": hi_at[h]}, device_id_type=MESH)
    if n_lo == 2:
        sibling = hi * 2 + (1 - lo)
        pl.semaphore_signal(barrier, inc=1, device_id={"dp": sibling}, device_id_type=MESH)
    for copy in mine:
        copy.wait()

    token = lax.broadcasted_iota(jnp.int32, (seq, LANES), 0)
    lane = lax.broadcasted_iota(jnp.int32, (ex, LANES), 1)

    def module_tile(j):
        columns = pl.ds(pl.multiple_of(j * LANES, LANES), LANES)
        for e in range(ex):
            grad = grad_v[e, :, columns].astype(jnp.float32)
            grad = jnp.where(token < lens_ref[e], grad, 0.0).astype(jnp.bfloat16)
            prod[pl.ds(e * LANES, LANES), :] = lax.dot_general(
                grad, act_v[e, :, columns], (((0,), (0,)), ((), ())),
                preferred_element_type=jnp.float32)
        for mm in range(per_tile):
            rows = []
            for t in range(tiles):
                row = None
                for k in range(per_tile):
                    part = prod[pl.ds(mm * rank + t * per_tile + k, ex, stride=LANES), :]
                    shift = (k - mm) % per_tile
                    if shift:
                        part = pltpu.roll(part, shift * rank, 1)
                    row = part if k == 0 else jnp.where(lane >= k * rank, part, row)
                rows.append(row)
            top = functools.reduce(jnp.maximum, [jnp.abs(row) for row in rows])
            power = jnp.ceil(jnp.log2(jnp.maximum(top, 1e-30) * (1.0 / 32766.0)))
            scale = jnp.exp2(-power)
            slot = j * per_tile + mm
            for t in range(tiles):
                coded[slot, :, t * LANES:(t + 1) * LANES] = (
                    jnp.round(rows[t] * scale).astype(jnp.int32).astype(jnp.int16))
            coded[slot, :, entries:] = power.astype(jnp.int32).astype(jnp.int16)

    if width == LANES:
        module_tile(0)
    else:
        lax.fori_loop(0, width // LANES, lambda j, c: (module_tile(j), c)[1], 0)

    peers = (n_mod - 1) + (n_hi - 1) + (n_lo - 1)
    pl.semaphore_wait(barrier, peers)

    def source(position):
        found = jnp.int32(0)
        for m in range(n_mod):
            found = jnp.where(assign_ref[m] == position, m, found)
        return found

    def slot_of(dp_index, mod_index):
        return dp_index * n_mod + mod_index

    def remote(src, dst, send, recv, device):
        return pltpu.make_async_remote_copy(
            src_ref=src, dst_ref=dst, send_sem=send, recv_sem=recv,
            device_id=device, device_id_type=MESH)

    started = []
    z_copies = [None] * n_mod
    for o in list(range(1, n_mod)) + [0]:
        block = coded[source(mod_at[o])]
        if o == 0:
            inbox[slot_of(dp, mod)] = block
        else:
            outbox[o] = block
            z_copies[o] = remote(outbox.at[o], inbox.at[slot_of(dp, mod)],
                                 z_send.at[o], z_recv.at[o], {"mod": mod_at[o]})
            z_copies[o].start()
            started.append(z_copies[o])

    def decode(position, block):
        def tile(t):
            columns = pl.ds(pl.multiple_of(t * LANES, LANES), LANES)
            value = inbox[block, :, columns].astype(jnp.int32).astype(jnp.float32)
            power = inbox[block, :, entries:].astype(jnp.int32).astype(jnp.float32)
            value = value * jnp.exp2(power)
            top = value.astype(jnp.bfloat16)
            rows = pl.ds(position * ex, ex)
            high[rows, columns] = top
            low[rows, columns] = (value - top.astype(jnp.float32)).astype(jnp.bfloat16)
        if small:
            for t in range(tiles):
                tile(t)
        else:
            lax.fori_loop(0, tiles, lambda t, c: (tile(t), c)[1], 0)

    out_rows = out_ref.shape[0] // tiles
    depth = n_lo * n_mod * ex
    inverse_count = 1.0 / (ex * n_mod * n_dp)

    def multiply(h):
        deep = pl.ds(h * depth, depth)
        left = pl.ds(pl.multiple_of(dp * out_rows, LANES), out_rows)
        left_high = high[deep, left].T
        left_low = low[deep, left].T

        def column(t):
            columns = pl.ds(pl.multiple_of(t * LANES, LANES), LANES)
            dot = functools.partial(jnp.dot, preferred_element_type=jnp.float32)
            total = (dot(left_high, high[deep, columns]) + dot(left_high, low[deep, columns])
                     + dot(left_low, high[deep, columns]))
            place = pl.ds(t, out_rows, stride=tiles)
            if h > 0:
                total = total + out_ref[place, :]
            if h == n_hi - 1:
                total = total * inverse_count
            out_ref[place, :] = total
        if small:
            for t in range(tiles):
                column(t)
        else:
            lax.fori_loop(0, tiles, lambda t, c: (column(t), c)[1], 0)

    x_copies = [[None] * n_mod for _ in range(n_hi)]
    c_copies = [None] * n_mod
    f_copies = [[None] * n_mod for _ in range(n_hi)]
    for o in range(n_mod):
        if o:
            z_copies[o].wait_recv()
        block = slot_of(dp, mod_from[o])
        for h in range(1, n_hi):
            x_copies[h][o] = remote(inbox.at[block], inbox.at[block],
                                    x_send.at[h, o], x_recv.at[h, o], {"dp": hi_at[h]})
            x_copies[h][o].start()
            started.append(x_copies[h][o])
        if n_lo == 2:
            c_copies[o] = remote(inbox.at[block], inbox.at[block],
                                 c_send.at[o], c_recv.at[o], {"dp": sibling})
            c_copies[o].start()
            started.append(c_copies[o])
        decode(o, block)
    if n_lo == 2:
        for o in range(n_mod):
            for h in range(1, n_hi):
                x_copies[h][o].wait_recv()
                block = slot_of(hi_from[h] * n_lo + lo, mod_from[o])
                f_copies[h][o] = remote(inbox.at[block], inbox.at[block],
                                        f_send.at[h, o], f_recv.at[h, o], {"dp": sibling})
                f_copies[h][o].start()
                started.append(f_copies[h][o])
            c_copies[o].wait_recv()
            decode(n_mod + o, slot_of(sibling, mod_from[o]))
    multiply(0)
    for h in range(1, n_hi):
        for o in range(n_mod):
            if n_lo == 1:
                x_copies[h][o].wait_recv()
            decode(h * n_lo * n_mod + o, slot_of(hi_from[h] * n_lo + lo, mod_from[o]))
        if n_lo == 2:
            for o in range(n_mod):
                f_copies[h][o].wait_recv()
                decode((h * n_lo + 1) * n_mod + o, slot_of(hi_from[h] * 2 + (1 - lo), mod_from[o]))
        multiply(h)
    for copy in started:
        copy.wait_send()


def solution(mesh):
    n_mod, n_dp = mesh.shape["mod"], mesh.shape["dp"]

    def body(act_proj, grad_proj, lengths, assignment):
        ex, seq, width = act_proj.shape
        rank = width // assignment.shape[0]
        entries = rank * rank
        out_rows = entries // n_dp
        tiles = entries // LANES
        n_hi = n_dp // 2 if n_dp % 2 == 0 else n_dp
        dma = pltpu.SemaphoreType.DMA
        any_spec = pl.BlockSpec(memory_space=pl.ANY)
        smem = pl.BlockSpec(memory_space=pltpu.SMEM)
        result = pl.pallas_call(
            functools.partial(kernel, n_mod, n_dp, rank),
            out_shape=jax.ShapeDtypeStruct((out_rows * tiles, LANES), jnp.float32),
            in_specs=[smem, smem, any_spec, any_spec],
            out_specs=pl.BlockSpec(memory_space=pltpu.VMEM),
            scratch_shapes=[
                pltpu.VMEM(act_proj.shape, jnp.bfloat16),
                pltpu.VMEM(grad_proj.shape, jnp.bfloat16),
                pltpu.VMEM((ex * LANES, LANES), jnp.float32),
                pltpu.VMEM((n_mod, ex, entries + LANES), jnp.int16),
                pltpu.VMEM((n_mod, ex, entries + LANES), jnp.int16),
                pltpu.VMEM((n_dp * n_mod, ex, entries + LANES), jnp.int16),
                pltpu.VMEM((n_dp * n_mod * ex, entries), jnp.bfloat16),
                pltpu.VMEM((n_dp * n_mod * ex, entries), jnp.bfloat16),
                dma((2,)),
                dma((n_mod,)), dma((n_mod,)),
                dma((n_hi, n_mod)), dma((n_hi, n_mod)),
                dma((n_mod,)), dma((n_mod,)),
                dma((n_hi, n_mod)), dma((n_hi, n_mod)),
            ],
            compiler_params=pltpu.CompilerParams(
                collective_id=0, has_side_effects=True, vmem_limit_bytes=48 * 1024 * 1024),
        )(lengths, assignment, act_proj, grad_proj)
        return result.reshape(out_rows, 1, entries)

    return jax.shard_map(
        body,
        mesh=mesh,
        in_specs=(
            P(("grp", "mod", "dp"), None, None),
            P(("grp", "mod", "dp"), None, None),
            P(("grp", "mod", "dp")),
            P(),
        ),
        out_specs=P(("grp", "dp"), "mod", None),
        check_vma=False,
    )
```

time: 87.9 us -> 19.6 us (0.22)
  waiting for transfers between devices: 43.8 us -> 0 us
  Pallas kernels: 0 us -> 15.2 us
  blocking collectives: 15 us -> 0 us
  between operations: 13.5 us -> 0.01 us
  matrix products: 5.44 us -> 0 us
  other arithmetic: 3.65 us -> 0 us
  local copies, waits for them, and re-layouts: 6.3 us -> 4.18 us
    reduce_scatter x1 -> x0, waiting for transfers between devices: 43.8 us -> none  [body(): lax.psum_scatter(jnp.einsum('emi,emj->imj', example_grad, example_grad, p...]
    pallas_call x0 -> x1, Pallas kernels: none -> 15.2 us  [body(): pl.pallas_call(functools.partial(kernel, n_mod, n_dp, rank), out_shape=ja...]
    all_to_all x1 -> x0, blocking collectives: 15 us -> none  [body(): lax.all_to_all(local_grad, 'mod', split_axis=1, concat_axis=0, tiled=True)]
    dot_general x2 -> x0, matrix products: 5.44 us -> none  [the longest x1 5.05 us: body(): jnp.einsum('emi,emj->imj', example_grad, example_grad, precision=lax.Prec...]
    mul x1 -> x0, local copies, waits for them, and re-layouts: 1.9 us -> none  [body(): return covariance * inverse_count]
    unnamed x2 -> x9, local copies, waits for them, and re-layouts: 2.45 us -> 4.18 us
    sort x1 -> x0, other arithmetic: 1.4 us -> none  [body(): source = jnp.argsort(assignment)]
    gather x2 -> x0, local copies, waits for them, and re-layouts: 1.3 us -> none  [the longest x1 0.65 us: body(): activations = jnp.take(activations, source, axis=2)]
  transfers between devices with their start and end apart: 1 -> 0, of which waited for: 1 -> 0; matrix products, arithmetic and copies ran while one was open for 0% -> 0% of each run, Pallas kernels for 0% -> 0%
where the time goes in v1:
time: 19.6 us; the launch traced here: 19.4 us
  Pallas kernels  15.2 us (78%)
  local copies, waits for them, and re-layouts  4.18 us (21%)
    pallas_call x1, Pallas kernels, body(): pl.pallas_call(functools.partial(kernel, n_mod, n_dp, rank), out_shape=ja...  15.2 us
    unnamed x9, local copies, waits for them, and re-layouts  4.18 us

profile of v1, /device:TPU:0, one launch (start us, length us, event | category | flops | bytes accessed | tf_op | source)
XLA Modules:
  0.0 19.4 jit_solution(17224299861828609420)
XLA Ops:
  0.0 0.0 copy-start
  0.0 0.9 %copy-done = bf16[16,64,128]{2,1,0:T(8,128)(2,1)S(1)} copy-done((bf16[16,64,128]{2,1,0:T(8,128)(2,1)S(1)}, bf16[16,64,128]{2,1,0:T(8,128)(2,1)}, u32[]{:S(2)}) %copy-start) | copy-done | bytes 262168
  1.0 0.0 copy-start.1
  1.0 0.9 %copy-done.1 = bf16[16,64,128]{2,1,0:T(8,128)(2,1)S(1)} copy-done((bf16[16,64,128]{2,1,0:T(8,128)(2,1)S(1)}, bf16[16,64,128]{2,1,0:T(8,128)(2,1)}, u32[]{:S(2)}) %copy-start.1) | copy-done | bytes 262168
  1.9 0.0 copy-start.2
  1.9 0.7 %copy-done.2 = s32[16]{0:T(128)S(1)} copy-done((s32[16]{0:T(128)S(1)}, s32[16]{0:T(128)}, u32[]{:S(2)}) %copy-start.2) | copy-done | bytes 88
  2.6 0.0 copy-start.3
  2.6 0.7 %copy-done.3 = s32[4]{0:T(128)S(1)} copy-done((s32[4]{0:T(128)S(1)}, s32[4]{0:T(128)}, u32[]{:S(2)}) %copy-start.3) | copy-done | bytes 40
  3.2 15.2 %shard_map.46 = f32[2048,128]{1,0:T(8,128)S(1)} custom-call(s32[16]{0:T(128)S(1)} %copy-done.2, s32[4]{0:T(128)S(1)} %copy-done.3, bf16[16,64,128]{2,1,0:T(8,128)(2,1)S(1)} %copy-done, bf16[16,64,128]{2,1,0:T(8,128)(2,1)S(1)} %copy-done.1), custom_call_target="tpu_custom_call" | custom-call | tf_op jit(solution)/shard_map/pallas_call | solution.py:216
  18.4 1.0 %copy.7 = f32[256,1,1024]{2,1,0:T(1,128)} copy(f32[256,1,1024]{2,1,0:T(1,128)S(1)} %bitcast.1) | data formatting | bytes 2097152
Async XLA Ops:
  0.0 0.9 %copy-start = (bf16[16,64,128]{2,1,0:T(8,128)(2,1)S(1)}, bf16[16,64,128]{2,1,0:T(8,128)(2,1)}, u32[]{:S(2)}) copy-start(bf16[16,64,128]{2,1,0:T(8,128)(2,1)} %act_hbm.1) | copy-start | bytes 786436
  1.0 0.9 %copy-start.1 = (bf16[16,64,128]{2,1,0:T(8,128)(2,1)S(1)}, bf16[16,64,128]{2,1,0:T(8,128)(2,1)}, u32[]{:S(2)}) copy-start(bf16[16,64,128]{2,1,0:T(8,128)(2,1)} %grad_hbm.1) | copy-start | bytes 786436
  1.9 0.7 %copy-start.2 = (s32[16]{0:T(128)S(1)}, s32[16]{0:T(128)}, u32[]{:S(2)}) copy-start(s32[16]{0:T(128)} %lens_ref.1) | copy-start | bytes 196
  2.6 0.7 %copy-start.3 = (s32[4]{0:T(128)S(1)}, s32[4]{0:T(128)}, u32[]{:S(2)}) copy-start(s32[4]{0:T(128)} %assign_ref.1) | copy-start | bytes 52

commit v2 on v1

--- a/solution.py
+++ b/solution.py
@@ -12,8 +12,8 @@
 
 
 def kernel(
-    n_mod, n_dp, rank, lens_ref, assign_ref, act_hbm, grad_hbm, out_ref,
-    act_v, grad_v, prod, coded, outbox, inbox, high, low,
+    n_mod, n_dp, rank, lens_hbm, assign_hbm, act_hbm, grad_hbm, out_ref,
+    lens_ref, assign_ref, act_v, grad_v, prod, coded, outbox, inbox, high, low,
     in_sem, z_send, z_recv, x_send, x_recv, c_send, c_recv, f_send, f_recv,
 ):
     ex, seq, width = act_v.shape
@@ -27,7 +27,9 @@
     dp = lax.axis_index("dp")
     hi, lo = dp // n_lo, dp % n_lo
     mine = [pltpu.make_async_copy(act_hbm, act_v, in_sem.at[0]),
-            pltpu.make_async_copy(grad_hbm, grad_v, in_sem.at[1])]
+            pltpu.make_async_copy(grad_hbm, grad_v, in_sem.at[1]),
+            pltpu.make_async_copy(lens_hbm, lens_ref, in_sem.at[2]),
+            pltpu.make_async_copy(assign_hbm, assign_ref, in_sem.at[3])]
     for copy in mine:
         copy.start()
 
@@ -211,14 +213,15 @@
         tiles = entries // LANES
         n_hi = n_dp // 2 if n_dp % 2 == 0 else n_dp
         dma = pltpu.SemaphoreType.DMA
-        any_spec = pl.BlockSpec(memory_space=pl.ANY)
-        smem = pl.BlockSpec(memory_space=pltpu.SMEM)
+        in_hbm = pl.BlockSpec(memory_space=pltpu.HBM)
         result = pl.pallas_call(
             functools.partial(kernel, n_mod, n_dp, rank),
             out_shape=jax.ShapeDtypeStruct((out_rows * tiles, LANES), jnp.float32),
-            in_specs=[smem, smem, any_spec, any_spec],
+            in_specs=[in_hbm] * 4,
             out_specs=pl.BlockSpec(memory_space=pltpu.VMEM),
             scratch_shapes=[
+                pltpu.SMEM(lengths.shape, jnp.int32),
+                pltpu.SMEM(assignment.shape, jnp.int32),
                 pltpu.VMEM(act_proj.shape, jnp.bfloat16),
                 pltpu.VMEM(grad_proj.shape, jnp.bfloat16),
                 pltpu.VMEM((ex * LANES, LANES), jnp.float32),
@@ -227,7 +230,7 @@
                 pltpu.VMEM((n_dp * n_mod, ex, entries + LANES), jnp.int16),
                 pltpu.VMEM((n_dp * n_mod * ex, entries), jnp.bfloat16),
                 pltpu.VMEM((n_dp * n_mod * ex, entries), jnp.bfloat16),
-                dma((2,)),
+                dma((4,)),
                 dma((n_mod,)), dma((n_mod,)),
                 dma((n_hi, n_mod)), dma((n_hi, n_mod)),
                 dma((n_mod,)), dma((n_mod,)),
@@ -235,7 +238,8 @@
             ],
             compiler_params=pltpu.CompilerParams(
                 collective_id=0, has_side_effects=True, vmem_limit_bytes=48 * 1024 * 1024),
-        )(lengths, assignment, act_proj, grad_proj)
+        )(*[pltpu.with_memory_space_constraint(x, pltpu.HBM)
+            for x in (lengths, assignment, act_proj, grad_proj)])
         return result.reshape(out_rows, 1, entries)
 
     return jax.shard_map(

time: 19.6 us -> 16.6 us (0.85)
  local copies, waits for them, and re-layouts: 4.18 us -> 0.97 us
  Pallas kernels: 15.2 us -> 15.4 us
    unnamed x9 -> x1, local copies, waits for them, and re-layouts: 4.18 us -> 0.97 us
    pallas_call x1, Pallas kernels: 15.2 us -> 15.4 us  [body(): pl.pallas_call(functools.partial(kernel, n_mod, n_dp, rank), out_shape=ja...]
where the time goes in v2:
time: 16.6 us; the launch traced here: 16.4 us
  Pallas kernels  15.4 us (93%)
  local copies, waits for them, and re-layouts  0.97 us (6%)
    pallas_call x1, Pallas kernels, body(): pl.pallas_call(functools.partial(kernel, n_mod, n_dp, rank), out_shape=ja...  15.4 us
    unnamed x1, local copies, waits for them, and re-layouts  0.97 us

profile of v2, /device:TPU:0, one launch (start us, length us, event | category | flops | bytes accessed | tf_op | source)
XLA Modules:
  0.0 16.4 jit_solution(6589974919496972598)
XLA Ops:
  0.0 15.4 %shard_map.46 = f32[2048,128]{1,0:T(8,128)S(1)} custom-call(s32[16]{0:T(128)} %lens_hbm.1, s32[4]{0:T(128)} %assign_hbm.1, bf16[16,64,128]{2,1,0:T(8,128)(2,1)} %act_hbm.1, bf16[16,64,128]{2,1,0:T(8,128)(2,1)} %grad_hbm.1), custom_call_target="tpu_custom_call" | custom-call | tf_op jit(solution)/shard_map/pallas_call | solution.py:217
  15.4 1.0 %copy.7 = f32[256,1,1024]{2,1,0:T(1,128)} copy(f32[256,1,1024]{2,1,0:T(1,128)S(1)} %bitcast.1) | data formatting | bytes 2097152

commit v3 on v2

--- a/solution.py
+++ b/solution.py
@@ -23,6 +23,7 @@
     n_lo = 2 if n_dp % 2 == 0 else 1
     n_hi = n_dp // n_lo
     small = n_mod <= 8
+    direct = n_mod - 1
     mod = lax.axis_index("mod")
     dp = lax.axis_index("dp")
     hi, lo = dp // n_lo, dp % n_lo
@@ -33,16 +34,26 @@
     for copy in mine:
         copy.start()
 
-    mod_at = [lax.rem(mod + o, n_mod) for o in range(n_mod)]
-    mod_from = [lax.rem(mod + n_mod - o, n_mod) for o in range(n_mod)]
+    def by_distance(k):
+        upper = jnp.where(mod + k < n_mod, mod + k, n_mod - 1 - k)
+        lower = jnp.where(k <= mod, mod - k, k)
+        return jnp.where(mod >= n_mod // 2, upper, lower)
+
+    near = [mod] + [by_distance(k) for k in range(1, n_mod)]
     hi_at = [lax.rem(hi + h, n_hi) * n_lo + lo for h in range(n_hi)]
+
+    def across(dp_index):
+        return dp_index + 1 - 2 * lo
+
     hi_from = [lax.rem(hi + n_hi - h, n_hi) for h in range(n_hi)]
 
     barrier = pltpu.get_barrier_semaphore()
     for o in range(1, n_mod):
-        pl.semaphore_signal(barrier, inc=1, device_id={"mod": mod_at[o]}, device_id_type=MESH)
+        pl.semaphore_signal(barrier, inc=1, device_id={"mod": near[o]}, device_id_type=MESH)
     for h in range(1, n_hi):
         pl.semaphore_signal(barrier, inc=1, device_id={"dp": hi_at[h]}, device_id_type=MESH)
+        if n_lo == 2 and direct < n_mod:
+            pl.semaphore_signal(barrier, inc=1, device_id={"dp": across(hi_at[h])}, device_id_type=MESH)
     if n_lo == 2:
         sibling = hi * 2 + (1 - lo)
         pl.semaphore_signal(barrier, inc=1, device_id={"dp": sibling}, device_id_type=MESH)
@@ -85,7 +96,7 @@
     else:
         lax.fori_loop(0, width // LANES, lambda j, c: (module_tile(j), c)[1], 0)
 
-    peers = (n_mod - 1) + (n_hi - 1) + (n_lo - 1)
+    peers = (n_mod - 1) + (n_hi - 1) * (2 if n_lo == 2 and direct < n_mod else 1) + (n_lo - 1)
     pl.semaphore_wait(barrier, peers)
 
     def source(position):
@@ -104,14 +115,14 @@
 
     started = []
     z_copies = [None] * n_mod
-    for o in list(range(1, n_mod)) + [0]:
-        block = coded[source(mod_at[o])]
+    for o in range(n_mod - 1, -1, -1):
+        block = coded[source(near[o])]
         if o == 0:
             inbox[slot_of(dp, mod)] = block
         else:
             outbox[o] = block
             z_copies[o] = remote(outbox.at[o], inbox.at[slot_of(dp, mod)],
-                                 z_send.at[o], z_recv.at[o], {"mod": mod_at[o]})
+                                 z_send.at[o], z_recv.at[mod], {"mod": near[o]})
             z_copies[o].start()
             started.append(z_copies[o])
 
@@ -162,14 +173,20 @@
     c_copies = [None] * n_mod
     f_copies = [[None] * n_mod for _ in range(n_hi)]
     for o in range(n_mod):
+        block = slot_of(dp, near[o])
         if o:
-            z_copies[o].wait_recv()
-        block = slot_of(dp, mod_from[o])
+            remote(inbox.at[block], inbox.at[block], z_send.at[o], z_recv.at[near[o]],
+                   {"mod": near[o]}).wait_recv()
         for h in range(1, n_hi):
             x_copies[h][o] = remote(inbox.at[block], inbox.at[block],
                                     x_send.at[h, o], x_recv.at[h, o], {"dp": hi_at[h]})
             x_copies[h][o].start()
             started.append(x_copies[h][o])
+            if n_lo == 2 and o >= direct:
+                f_copies[h][o] = remote(inbox.at[block], inbox.at[block],
+                                        f_send.at[h, o], f_recv.at[h, o], {"dp": across(hi_at[h])})
+                f_copies[h][o].start()
+                started.append(f_copies[h][o])
         if n_lo == 2:
             c_copies[o] = remote(inbox.at[block], inbox.at[block],
                                  c_send.at[o], c_recv.at[o], {"dp": sibling})
@@ -179,24 +196,26 @@
     if n_lo == 2:
         for o in range(n_mod):
             for h in range(1, n_hi):
-                x_copies[h][o].wait_recv()
-                block = slot_of(hi_from[h] * n_lo + lo, mod_from[o])
-                f_copies[h][o] = remote(inbox.at[block], inbox.at[block],
-                                        f_send.at[h, o], f_recv.at[h, o], {"dp": sibling})
-                f_copies[h][o].start()
-                started.append(f_copies[h][o])
+                if o < direct:
+                    x_copies[h][o].wait_recv()
+                    block = slot_of(hi_from[h] * n_lo + lo, near[o])
+                    f_copies[h][o] = remote(inbox.at[block], inbox.at[block],
+                                            f_send.at[h, o], f_recv.at[h, o], {"dp": sibling})
+                    f_copies[h][o].start()
+                    started.append(f_copies[h][o])
             c_copies[o].wait_recv()
-            decode(n_mod + o, slot_of(sibling, mod_from[o]))
+            decode(n_mod + o, slot_of(sibling, near[o]))
     multiply(0)
     for h in range(1, n_hi):
         for o in range(n_mod):
-            if n_lo == 1:
+            if n_lo == 1 or o >= direct:
                 x_copies[h][o].wait_recv()
-            decode(h * n_lo * n_mod + o, slot_of(hi_from[h] * n_lo + lo, mod_from[o]))
-        if n_lo == 2:
-            for o in range(n_mod):
-                f_copies[h][o].wait_recv()
-                decode((h * n_lo + 1) * n_mod + o, slot_of(hi_from[h] * 2 + (1 - lo), mod_from[o]))
+            decode(h * n_lo * n_mod + o, slot_of(hi_from[h] * n_lo + lo, near[o]))
+            if n_lo == 2:
+                block = slot_of(hi_from[h] * 2 + (1 - lo), near[o])
+                remote(inbox.at[block], inbox.at[block], f_send.at[h, o], f_recv.at[h, o],
+                       {"dp": sibling}).wait_recv()
+                decode((h * n_lo + 1) * n_mod + o, block)
         multiply(h)
     for copy in started:
         copy.wait_send()

time: 16.6 us -> 15.4 us (0.928)
  Pallas kernels: 15.4 us -> 14.3 us
    pallas_call x1, Pallas kernels: 15.4 us -> 14.3 us  [body(): pl.pallas_call(functools.partial(kernel, n_mod, n_dp, rank), out_shape=ja...]
where the time goes in v3:
time: 15.4 us; the launch traced here: 15.3 us
  Pallas kernels  14.3 us (93%)
  local copies, waits for them, and re-layouts  0.97 us (6%)
    pallas_call x1, Pallas kernels, body(): pl.pallas_call(functools.partial(kernel, n_mod, n_dp, rank), out_shape=ja...  14.3 us
    unnamed x1, local copies, waits for them, and re-layouts  0.97 us

profile of v3, /device:TPU:0, one launch (start us, length us, event | category | flops | bytes accessed | tf_op | source)
XLA Modules:
  0.0 15.3 jit_solution(10338181582216328122)
XLA Ops:
  0.0 14.3 %shard_map.46 = f32[2048,128]{1,0:T(8,128)S(1)} custom-call(s32[16]{0:T(128)} %lens_hbm.1, s32[4]{0:T(128)} %assign_hbm.1, bf16[16,64,128]{2,1,0:T(8,128)(2,1)} %act_hbm.1, bf16[16,64,128]{2,1,0:T(8,128)(2,1)} %grad_hbm.1), custom_call_target="tpu_custom_call" | custom-call | tf_op jit(solution)/shard_map/pallas_call | solution.py:236
  14.3 1.0 %copy.7 = f32[256,1,1024]{2,1,0:T(1,128)} copy(f32[256,1,1024]{2,1,0:T(1,128)S(1)} %bitcast.1) | data formatting | bytes 2097152

commit v4 on v3

--- a/solution.py
+++ b/solution.py
@@ -151,12 +151,13 @@
         left = pl.ds(pl.multiple_of(dp * out_rows, LANES), out_rows)
         left_high = high[deep, left].T
         left_low = low[deep, left].T
+        left_all = jnp.concatenate([left_high, left_high, left_low], axis=1)
 
         def column(t):
             columns = pl.ds(pl.multiple_of(t * LANES, LANES), LANES)
-            dot = functools.partial(jnp.dot, preferred_element_type=jnp.float32)
-            total = (dot(left_high, high[deep, columns]) + dot(left_high, low[deep, columns])
-                     + dot(left_low, high[deep, columns]))
+            right_high = high[deep, columns]
+            right_all = jnp.concatenate([right_high, low[deep, columns], right_high], axis=0)
+            total = jnp.dot(left_all, right_all, preferred_element_type=jnp.float32)
             place = pl.ds(t, out_rows, stride=tiles)
             if h > 0:
                 total = total + out_ref[place, :]

time: 15.4 us -> 15.4 us (level)
  no operation moved by 1% of the time
where the time goes in v4:
time: 15.4 us; the launch traced here: 15.2 us
  Pallas kernels  14.3 us (93%)
  local copies, waits for them, and re-layouts  0.97 us (6%)
    pallas_call x1, Pallas kernels, body(): pl.pallas_call(functools.partial(kernel, n_mod, n_dp, rank), out_shape=ja...  14.3 us
    unnamed x1, local copies, waits for them, and re-layouts  0.97 us

profile of v4, /device:TPU:0, one launch (start us, length us, event | category | flops | bytes accessed | tf_op | source)
XLA Modules:
  0.0 15.2 jit_solution(15236811852846709262)
XLA Ops:
  0.0 14.3 %shard_map.46 = f32[2048,128]{1,0:T(8,128)S(1)} custom-call(s32[16]{0:T(128)} %lens_hbm.1, s32[4]{0:T(128)} %assign_hbm.1, bf16[16,64,128]{2,1,0:T(8,128)(2,1)} %act_hbm.1, bf16[16,64,128]{2,1,0:T(8,128)(2,1)} %grad_hbm.1), custom_call_target="tpu_custom_call" | custom-call | tf_op jit(solution)/shard_map/pallas_call | solution.py:237
  14.3 1.0 %copy.7 = f32[256,1,1024]{2,1,0:T(1,128)} copy(f32[256,1,1024]{2,1,0:T(1,128)S(1)} %bitcast.1) | data formatting | bytes 2097152
